TPU v7x, 128 devices: a whole 4x4x4 slice. The times are simulated.
128 devices in a mesh: section: 2 (over core), dp: 16 (over z, y), tensor: 4 (over x).
Axes of the slice: x: 4, y: 4, z: 4, core: 2. Of those that a mesh axis runs over, the one named last changes fastest.
Arguments:
- tokens: bfloat16 [32, 384, 1088], P('dp', 'tensor'), may hold values from -6 to 6
- cotangent: bfloat16 [32, 384, 1088], P('dp', 'tensor'), may hold values from -6 to 6
- doc_lengths: int32 [32, 4], P('dp'), may hold values from 1 to 336, 384 in all within a row
- norm_gains: bfloat16 [2, 2, 1088], P('section', None, 'tensor'), may hold values from 0.5 to 1.5
- w_qkv: bfloat16 [2, 1088, 3264], P('section', 'tensor'), may hold values from -0.1875 to 0.1875
- w_out: bfloat16 [2, 1088, 1088], P('section', 'tensor'), may hold values from -0.75 to 0.75
- w_up: bfloat16 [2, 1088, 4352], P('section', None, 'tensor'), may hold values from -0.1875 to 0.1875
- w_down: bfloat16 [2, 4352, 1088], P('section', 'tensor'), may hold values from -0.09375 to 0.09375
Outputs:
- activations: bfloat16 [2, 32, 384, 1088], P('section', 'dp', 'tensor')
- input_grads: bfloat16 [2, 32, 384, 1088], P('section', 'dp', 'tensor')
- grad_gains: float32 [2, 2, 1088], P('section', None, 'tensor')
- grad_qkv: float32 [2, 1088, 3264], P('section', 'tensor')
- grad_out: float32 [2, 1088, 1088], P('section', 'tensor')
- grad_up: float32 [2, 1088, 4352], P('section', None, 'tensor')
- grad_down: float32 [2, 4352, 1088], P('section', 'tensor')
Inputs may be any that keep to these rules, and one draw needn't show every extreme that they name: `doc_lengths`: each row holds the lengths of the 4 documents of one sequence, summing to 384; the longest has exactly 336 tokens.
All inputs are finite; a program needn't handle non-finite values.
Results may differ from a plain program's by a relative error of at most 0.035.
Values may be sent and summed in bfloat16 or wider, within the bound.
A program may use at most 192 MiB of HBM per device.

v0:
```python
import functools
import jax
import jax.numpy as jnp
from jax import lax
from jax.experimental import pallas as pl
from jax.experimental.pallas import tpu as pltpu
from jax.sharding import PartitionSpec as P

HEAD_DIM = 64
LOW = jnp.bfloat16
F32 = jnp.float32
MESH = pl.DeviceIdType.MESH


def dot_nn(left, right):
    return lax.dot_general(left, right, (((1,), (0,)), ((), ())), preferred_element_type=F32)


def dot_nt(left, right):
    return lax.dot_general(left, right, (((1,), (1,)), ((), ())), preferred_element_type=F32)


def dot_tn(left, right):
    return lax.dot_general(left, right, (((0,), (0,)), ((), ())), preferred_element_type=F32)


class Ring:
    def __init__(self, axis):
        whole = lax.axis_index("dp")
        rest = None
        if axis == "x":
            self.me = lax.axis_index("tensor")
        elif axis == "y":
            self.me, rest = lax.rem(whole, 4), lax.div(whole, 4) * 4
        else:
            self.me, rest = lax.div(whole, 4), lax.rem(whole, 4)
        self.right = lax.rem(self.me + 1, 4)
        self.left = lax.rem(self.me + 3, 4)
        self.opposite = lax.rem(self.me + 2, 4)

        def device(place):
            if axis == "x":
                return {"tensor": place}
            if axis == "y":
                return {"dp": rest + place}
            return {"dp": place * 4 + rest}

        self.to_right, self.to_left = device(self.right), device(self.left)
        self.to_opposite = device(self.opposite)


def sibling():
    return {"section": 1 - lax.axis_index("section")}


def greet(*targets):
    barrier = pltpu.get_barrier_semaphore()
    for target in targets:
        pl.semaphore_signal(barrier, inc=1, device_id=target, device_id_type=MESH)
    pl.semaphore_wait(barrier, len(targets))


def remote(src, dst, sems, which, target):
    return pltpu.make_async_remote_copy(
        src_ref=src,
        dst_ref=dst,
        send_sem=sems[0].at[which],
        recv_sem=sems[1].at[which],
        device_id=target,
        device_id_type=MESH,
    )


class Gather:
    def __init__(self, ring, slot, sems, own=None):
        self.ring, self.slot, self.sems = ring, slot, sems
        self.own = own if own is not None else lambda half: slot(ring.me, half)

    def copy(self, which, arriving=False):
        ring = self.ring
        half = (0, 1, 1, 0, 0, 1)[which]
        goes_right = which in (0, 2, 4)
        target = ring.to_right if goes_right else ring.to_left
        if which < 4:
            source_block = ring.left if goes_right else ring.right
            if not arriving:
                return remote(self.own(half), self.slot(ring.me, half), self.sems, which, target)
        else:
            source_block = ring.opposite
            if not arriving:
                handed = self.slot(ring.left if goes_right else ring.right, half)
                return remote(handed, handed, self.sems, which, target)
        part = self.slot(source_block, half)
        return remote(part, part, self.sems, which, target)

    def start(self):
        for which in range(4):
            self.copy(which).start()

    def relay(self):
        for which in (0, 1):
            self.copy(which, arriving=True).wait_recv()
            self.copy(which + 4).start()

    def wait_left(self):
        self.copy(2, arriving=True).wait_recv()

    def wait_right(self):
        self.copy(3, arriving=True).wait_recv()

    def wait_opposite(self):
        self.copy(4, arriving=True).wait_recv()
        self.copy(5, arriving=True).wait_recv()

    def wait_all(self):
        self.wait_left()
        self.wait_right()
        self.wait_opposite()

    def finish(self):
        for which in range(6):
            self.copy(which).wait_send()


class Scatter:
    def __init__(self, ring, part, landing, passing, arrived, sems):
        self.ring, self.part, self.landing, self.passing = ring, part, landing, passing
        self.arrived, self.sems = arrived, sems

    def copy(self, which):
        ring = self.ring
        half = (0, 1, 1, 0, 0, 1)[which]
        goes_right = which in (0, 2, 4)
        if which < 2:
            src, dst = self.part(ring.opposite, half), self.landing(half)
        else:
            dst = self.arrived(0 if goes_right else 1, half)
            if which < 4:
                src = self.part(ring.right if goes_right else ring.left, half)
            else:
                src = self.passing(half)
        return remote(src, dst, self.sems, which, ring.to_right if goes_right else ring.to_left)

    def start_near(self):
        self.copy(2).start()
        self.copy(3).start()

    def start_far(self):
        self.copy(0).start()
        self.copy(1).start()

    def relay(self):
        for half, block in ((0, self.ring.right), (1, self.ring.left)):
            self.copy(half).wait_recv()
            added = self.part(block, half)[...].astype(F32) + self.landing(half)[...].astype(F32)
            self.passing(half)[...] = added.astype(LOW)
            self.copy(half + 4).start()

    def wait(self):
        for which in (2, 3, 4, 5):
            self.copy(which).wait_recv()

    def total(self, half):
        return (
            self.part(self.ring.me, half)[...].astype(F32)
            + self.arrived(0, half)[...].astype(F32)
            + self.arrived(1, half)[...].astype(F32)
        )

    def finish(self):
        for which in range(6):
            self.copy(which).wait_send()


class DirectGather:
    def __init__(self, ring, slot, sems, own=None):
        self.ring, self.slot, self.sems = ring, slot, sems
        self.own = own if own is not None else lambda half: slot(ring.me, half)

    def copy(self, which):
        target = (self.ring.to_right, self.ring.to_left, self.ring.to_opposite)[which]
        return remote(self.own(None), self.slot(self.ring.me, None), self.sems, which, target)

    def start(self):
        for which in (2, 0, 1):
            self.copy(which).start()

    def relay(self):
        pass

    def wait_all(self):
        for which, block in enumerate((self.ring.left, self.ring.right, self.ring.opposite)):
            part = self.slot(block, None)
            remote(part, part, self.sems, which, self.ring.to_right).wait_recv()

    def finish(self):
        for which in range(3):
            self.copy(which).wait_send()


class DirectScatter:
    def __init__(self, ring, part, arrived, sems):
        self.ring, self.part, self.arrived, self.sems = ring, part, arrived, sems

    def copy(self, which):
        ring = self.ring
        block = (ring.right, ring.left, ring.opposite)[which]
        target = (ring.to_right, ring.to_left, ring.to_opposite)[which]
        return remote(self.part(block, None), self.arrived(which), self.sems, which, target)

    def start_far(self):
        self.copy(2).start()

    def start_near(self):
        self.copy(0).start()
        self.copy(1).start()

    def relay(self):
        pass

    def wait(self):
        for which in range(3):
            self.copy(which).wait_recv()

    def whole(self):
        near = self.arrived(0)[...].astype(F32) + self.arrived(1)[...].astype(F32)
        own = self.part(self.ring.me, None)[...].astype(F32)
        return (own + near) + self.arrived(2)[...].astype(F32)

    def finish(self):
        for which in range(3):
            self.copy(which).wait_send()


def row_gather(ring, full, sems, columns=slice(None)):
    half = full.shape[1] // 2
    return Gather(
        ring, lambda block, which: full.at[block, pl.ds(which * half, half), columns], sems
    )


def row_scatter(ring, parts, landing, passing, arrived, sems, columns=slice(None)):
    half = parts.shape[1] // 2

    def rows(which):
        return pl.ds(which * half, half)

    return Scatter(
        ring,
        lambda block, which: parts.at[block, rows(which), columns],
        lambda which: landing.at[which, :, columns],
        lambda which: passing.at[which, :, columns],
        lambda side, which: arrived.at[side, rows(which), columns],
        sems,
    )


def row_total(scatter):
    scatter.wait()
    return jnp.concatenate([scatter.total(0), scatter.total(1)], axis=0)


def head_groups(features):
    pairs = pair_columns(features)
    middle = (len(pairs) + 1) // 2
    begin = pairs[middle][0]
    return (
        (pl.ds(0, begin), pairs[:middle]),
        (pl.ds(begin, features - begin), pairs[middle:]),
    )


def norm_stats(values):
    average = jnp.mean(values, axis=-1, keepdims=True)
    centered = values - average
    variance = jnp.mean(centered * centered, axis=-1, keepdims=True)
    scale = lax.rsqrt(variance + 1e-05)
    return centered * scale, scale


def norm_back(values, gain, grad):
    xhat, scale = norm_stats(values)
    scaled = grad * gain
    part = scale * (
        scaled
        - jnp.mean(scaled, axis=-1, keepdims=True)
        - xhat * jnp.mean(scaled * xhat, axis=-1, keepdims=True)
    )
    return part, jnp.sum(grad * xhat, axis=0, keepdims=True)


def gelu_tanh(values):
    inner = 0.7978845608028654 * (values + 0.044715 * values * values * values)
    return 0.5 * values * (1.0 + jnp.tanh(inner))


def gelu_slope(values):
    square = values * values
    bent = jnp.tanh(0.7978845608028654 * values * (1.0 + 0.044715 * square))
    slope = 0.7978845608028654 * (1.0 + 3.0 * 0.044715 * square)
    return 0.5 * (1.0 + bent) + 0.5 * values * (1.0 - bent * bent) * slope


def pick_copies(layer, mine, theirs, target, sem):
    def start():
        mine_here = lax.axis_index("section") == layer

        @pl.when(mine_here)
        def _():
            pltpu.make_async_copy(mine, target, sem).start()

        @pl.when(jnp.logical_not(mine_here))
        def _():
            pltpu.make_async_copy(theirs, target, sem).start()

    def wait():
        pltpu.make_async_copy(mine, target, sem).wait()

    return start, wait


def pair_columns(features):
    width = 2 * HEAD_DIM
    return [
        (start, min(width, features - start)) for start in range(0, features, width)
    ]


def head_masks(width):
    lanes = lax.broadcasted_iota(jnp.int32, (1, width), 1)
    if width == HEAD_DIM:
        return [None]
    return [lanes < HEAD_DIM, lanes >= HEAD_DIM]


def masked(values, mask):
    return values if mask is None else jnp.where(mask, values, jnp.zeros_like(values))


def plain_copy(src, target, sem):
    copy = functools.partial(pltpu.make_async_copy, src, target, sem)
    return lambda: copy().start(), lambda: copy().wait()


def forward_kernel(layer, features, *refs):
    take = iter(refs)

    def some(count):
        return [next(take) for _ in range(count)]

    (x_ref, bias_ref, gains_ref, at_full, up_mine, up_theirs, down_mine, down_theirs) = some(8)
    shard_ref = next(take) if layer == 0 else None
    (y_ref, middle_ref, one_ref, query_ref, key_ref, value_ref, mixed_ref, two_ref, act_ref,
     hidden_ref) = some(10)
    next_ref = next(take) if layer == 0 else None
    (at_w, up_w, down_w, weight_sems_, parts, landing, passing, arrived,
     key_send, key_recv, value_send, value_recv, two_send, two_recv, sum_send, sum_recv) = some(16)
    ring = Ring("x")
    me = ring.me
    fetches = [
        plain_copy(at_full.at[which], at_w.at[which], weight_sems_.at[which]) for which in range(4)
    ]
    fetches.append(pick_copies(layer, up_mine, up_theirs, up_w, weight_sems_.at[4]))
    fetches.append(pick_copies(layer, down_mine, down_theirs, down_w, weight_sems_.at[5]))
    for which in (1, 2, 0, 3, 4, 5):
        fetches[which][0]()
    if layer == 0:
        following = WeightGather(1, shard_ref, next_ref, (0, 144, 80, 64), some(13))
        greet_all()
    else:
        greet(ring.to_right, ring.to_left)

    def steps(*names):
        if layer == 0:
            following.steps(*names)

    rows = x_ref.shape[0]
    inputs = x_ref[...].astype(F32)
    xhat, _ = norm_stats(inputs)
    one_ref[...] = (xhat * gains_ref[0:1, :]).astype(LOW)
    normed_one = one_ref[...]
    groups = head_groups(features)
    keys, values = [], []
    fetches[1][1]()
    fetches[2][1]()
    for which, (columns, _) in enumerate(groups):
        key_ref[me, :, columns] = dot_nn(normed_one, at_w[1, :, columns]).astype(LOW)
        keys.append(
            row_gather(ring, key_ref, (key_send.at[which], key_recv.at[which]), columns)
        )
        if which == 0:
            keys[0].start()
        value_ref[me, :, columns] = dot_nn(normed_one, at_w[2, :, columns]).astype(LOW)
        values.append(
            row_gather(ring, value_ref, (value_send.at[which], value_recv.at[which]), columns)
        )
        if which == 0:
            values[0].start()
            steps("start")
    fetches[0][1]()
    query_ref[...] = dot_nn(normed_one, at_w[0]).astype(LOW)
    keys[0].relay()
    values[0].relay()
    keys[1].start()
    values[1].start()
    steps("first_relay")
    bias = bias_ref[...]

    def attend(begin, width):
        columns = pl.ds(begin, width)
        queries = query_ref[:, columns]
        key_block = key_ref[:, :, columns].reshape(4 * rows, width)
        value_block = value_ref[:, :, columns].reshape(4 * rows, width)
        mixed = None
        for mask in head_masks(width):
            scores = dot_nt(masked(queries, mask), key_block) * 0.125 + bias
            raised = jnp.exp(scores - jnp.max(scores, axis=-1, keepdims=True))
            probs = raised * (1.0 / jnp.sum(raised, axis=-1, keepdims=True))
            own = dot_nn(probs.astype(LOW), value_block)
            mixed = own if mixed is None else jnp.where(mask, own, mixed)
        mixed_ref[:, columns] = mixed.astype(LOW)

    for which, (_, pairs) in enumerate(groups):
        keys[which].wait_all()
        values[which].wait_all()
        for count, (begin, width) in enumerate(pairs):
            attend(begin, width)
            if which == 0 and count == 2:
                keys[1].relay()
                values[1].relay()
                steps("second")
    fetches[3][1]()
    middle_ref[...] = x_ref[...].astype(F32) + dot_nn(mixed_ref[...], at_w[3])
    xhat, _ = norm_stats(middle_ref[...])
    two_ref[me] = (xhat * gains_ref[1:2, :]).astype(LOW)
    tokens = row_gather(ring, two_ref, (two_send, two_recv))
    tokens.start()
    fetches[4][1]()
    fetches[5][1]()
    sums = row_scatter(ring, parts, landing, passing, arrived, (sum_send, sum_recv))

    def feed(block):
        act_ref[block] = dot_nn(two_ref[block], up_w[...])
        hidden_ref[block] = gelu_tanh(act_ref[block]).astype(LOW)
        parts[block] = dot_nn(hidden_ref[block], down_w[...]).astype(LOW)

    feed(me)
    tokens.relay()
    tokens.wait_left()
    feed(ring.left)
    tokens.wait_right()
    feed(ring.right)
    sums.start_near()
    tokens.wait_opposite()
    feed(ring.opposite)
    sums.start_far()
    sums.relay()
    steps("second_relay")
    y_ref[...] = (middle_ref[...] + row_total(sums)).astype(LOW)
    for gather in keys + values:
        gather.finish()
    tokens.finish()
    sums.finish()
    if layer == 0:
        following.end()


def scatter_scratch(rows, features):
    return [
        pltpu.VMEM((4, rows, features), LOW),
        pltpu.VMEM((2, rows // 2, features), LOW),
        pltpu.VMEM((2, rows // 2, features), LOW),
        pltpu.VMEM((2, rows, features), LOW),
    ]


def weight_scratch(features, hidden, matrices=4):
    shape = (features, features) if matrices == 1 else (matrices, features, features)
    return [
        pltpu.VMEM(shape, LOW),
        pltpu.VMEM((features, hidden), LOW),
        pltpu.VMEM((hidden, features), LOW),
        pltpu.SemaphoreType.DMA((6,)),
    ]


def in_vmem():
    return pl.BlockSpec(memory_space=pltpu.VMEM)


def anywhere():
    return pl.BlockSpec(memory_space=pl.ANY)


def forward_layer(layer, x, bias, gains, attention, feed, shard=()):
    rows, features = x.shape
    hidden = feed[0].shape[1]
    out_shape = (
        jax.ShapeDtypeStruct((rows, features), LOW),
        jax.ShapeDtypeStruct((rows, features), F32),
        jax.ShapeDtypeStruct((rows, features), LOW),
        jax.ShapeDtypeStruct((rows, features), LOW),
        jax.ShapeDtypeStruct((4, rows, features), LOW),
        jax.ShapeDtypeStruct((4, rows, features), LOW),
        jax.ShapeDtypeStruct((rows, features), LOW),
        jax.ShapeDtypeStruct((4, rows, features), LOW),
        jax.ShapeDtypeStruct((4, rows, hidden), F32),
        jax.ShapeDtypeStruct((4, rows, hidden), LOW),
    )
    following = (
        (jax.ShapeDtypeStruct((4, 4, features // 4, features), LOW),) if layer == 0 else ()
    )
    return pl.pallas_call(
        functools.partial(forward_kernel, layer, features),
        out_shape=out_shape + following,
        in_specs=[in_vmem()] * 3 + [anywhere()] * (5 + len(shard)),
        out_specs=[in_vmem()] * len(out_shape) + [anywhere()] * len(following),
        scratch_shapes=weight_scratch(features, hidden)
        + scatter_scratch(rows, features)
        + [pltpu.SemaphoreType.DMA((2, 6))] * 4
        + [pltpu.SemaphoreType.DMA((6,))] * 4
        + (weight_sems() if layer == 0 else []),
        compiler_params=pltpu.CompilerParams(
            collective_id=layer, has_side_effects=True, vmem_limit_bytes=56 * 2**20
        ),
        cost_estimate=pl.CostEstimate(
            flops=3 * 10**9, bytes_accessed=24 * 10**6, transcendentals=10**6
        ),
        name=f"layer_forward_{layer}",
    )(x, bias, gains, attention, *feed, *shard)


def backward_kernel(layer, features, *refs):
    take = iter(refs)

    def some(count):
        return [next(take) for _ in range(count)]

    (x_ref, dy_ref, bias_ref, gains_ref, middle_ref, query_ref, key_ref, value_ref, act_ref,
     at_full, up_mine, up_theirs, down_mine, down_theirs) = some(14)
    operands = some(12) if layer == 0 else None
    (dx_ref, gain_ref, out_ref, pre_ref, branch_ref, dquery_ref, dkey_ref, dvalue_ref) = some(8)
    results = some(4) if layer == 0 else None
    (at_w, up_w, down_w, weight_sems, parts, landing, passing, arrived, parts_b, landing_b,
     passing_b, arrived_b, parts_c, landing_c, passing_c, arrived_c, mixed_grad, kept_grad,
     out_send, out_recv, sum_send, sum_recv, key_send, key_recv, value_send, value_recv) = some(26)
    extra = layer == 0
    if extra:
        (two, pre, hidden, out_all, one, mixed, dq, dk, dv, branch, two_own, hidden_own) = operands
        feed_out, feed_given, feed_own_out, kept = results
        feed_one = FeedSum(features, (two, pre, hidden, out_all), feed_out, take)
        feed_own = FeedSum(
            features, (two_own, pre_ref, hidden_own, out_ref), feed_own_out, take
        )
        across = AcrossSum(features, (one, mixed, dq, dk, dv, branch), kept, take)
        given = hand_over(1, feed_out, feed_given, feed_one.end_sems)
    ring = Ring("x")
    me = ring.me
    fetches = [
        plain_copy(at_full.at[which], target, weight_sems.at[which])
        for which, target in enumerate((up_w, down_w, at_w, at_w))
    ]
    fetches.append(pick_copies(layer, up_mine, up_theirs, up_w, weight_sems.at[4]))
    fetches.append(pick_copies(layer, down_mine, down_theirs, down_w, weight_sems.at[5]))
    for which in (5, 4, 3):
        fetches[which][0]()
    rows = x_ref.shape[0]
    out_ref[me] = dy_ref[...]
    if not extra:
        greet(ring.to_right, ring.to_left)
    else:
        greet_all()
    grads = row_gather(ring, out_ref, (out_send, out_recv))
    grads.start()
    if extra:
        across.inputs.start()
        feed_one.inputs.start()
    sums = row_scatter(ring, parts, landing, passing, arrived, (sum_send, sum_recv))
    fetches[5][1]()
    fetches[4][1]()

    def feed(block):
        hidden_grad = dot_nt(out_ref[block], down_w[...])
        pre_ref[block] = (hidden_grad * gelu_slope(act_ref[block])).astype(LOW)
        parts[block] = dot_nt(pre_ref[block], up_w[...]).astype(LOW)

    feed(me)
    grads.relay()
    if extra:
        across.products(0)
        feed_one.products()
    grads.wait_left()
    feed(ring.left)
    grads.wait_right()
    feed(ring.right)
    sums.start_near()
    grads.wait_opposite()
    feed(ring.opposite)
    sums.start_far()
    for which in (0, 1):
        fetches[which][0]()
    if extra:
        feed_own.inputs.start()
        feed_one.run("relay")
    sums.relay()
    if extra:
        across.products(1)
    middle_part, gain_two = norm_back(middle_ref[...], gains_ref[1:2, :], row_total(sums))
    gain_ref[1:2, :] = gain_two
    middle_grad = dy_ref[...].astype(F32) + middle_part
    kept_grad[...] = middle_grad
    branch_ref[...] = middle_grad.astype(LOW)
    fetches[3][1]()
    mixed_grad[...] = dot_nt(branch_ref[...], at_w[...]).astype(LOW)
    fetches[2][0]()
    bias = bias_ref[...]
    groups = head_groups(features)
    dkeys = [
        row_scatter(ring, parts_b, landing_b, passing_b, arrived_b,
                    (key_send.at[which], key_recv.at[which]), columns)
        for which, (columns, _) in enumerate(groups)
    ]
    dvalues = [
        row_scatter(ring, parts_c, landing_c, passing_c, arrived_c,
                    (value_send.at[which], value_recv.at[which]), columns)
        for which, (columns, _) in enumerate(groups)
    ]

    def send_pair(which):
        for scatter in (dkeys[which], dvalues[which]):
            scatter.start_far()
        for scatter in (dkeys[which], dvalues[which]):
            scatter.start_near()

    def relay_pair(which):
        for scatter in (dkeys[which], dvalues[which]):
            scatter.relay()

    for count, (begin, width) in enumerate(pair_columns(features)):
        columns = pl.ds(begin, width)
        queries = query_ref[:, columns]
        outer = mixed_grad[:, columns]
        key_block = key_ref[:, :, columns].reshape(4 * rows, width)
        value_block = value_ref[:, :, columns].reshape(4 * rows, width)
        dquery = dkey = dvalue = None
        for mask in head_masks(width):
            query_one, outer_one = masked(queries, mask), masked(outer, mask)
            scores = dot_nt(key_block, query_one) * 0.125 + bias
            raised = jnp.exp(scores - jnp.max(scores, axis=0, keepdims=True))
            probs = raised * (1.0 / jnp.sum(raised, axis=0, keepdims=True))
            probs_grad = dot_nt(value_block, outer_one)
            mean = jnp.sum(probs * probs_grad, axis=0, keepdims=True)
            score_grad = (probs * (probs_grad - mean)).astype(LOW)
            own_query = dot_tn(score_grad, key_block)
            own_key = dot_nn(score_grad, query_one)
            own_value = dot_nn(probs.astype(LOW), outer_one)
            if dquery is None:
                dquery, dkey, dvalue = own_query, own_key, own_value
            else:
                dquery = jnp.where(mask, own_query, dquery)
                dkey, dvalue = dkey + own_key, dvalue + own_value
        dquery_ref[:, columns] = (dquery * 0.125).astype(LOW)
        parts_b[:, :, columns] = (dkey * 0.125).astype(LOW).reshape(4, rows, width)
        parts_c[:, :, columns] = dvalue.astype(LOW).reshape(4, rows, width)
        if begin + width == groups[0][0].size:
            send_pair(0)
        if extra and count == 1:
            feed_one.run("middle")
            across.relay(0)
        if extra and count == 4:
            feed_own.products()
            feed_one.run("middle_relay")
        if extra and count == 7:
            feed_own.run("relay")
    relay_pair(0)
    send_pair(1)
    for which in (0, 1, 2):
        fetches[which][1]()
    one_grad = dot_nt(dquery_ref[...], up_w[...])
    if extra:
        feed_one.run("end")
    relay_pair(1)
    if extra:
        across.relay(1)
        feed_own.run("middle")
        feed_one.run("end_relay")
    for which, (columns, _) in enumerate(groups):
        dkey_ref[:, columns] = row_total(dkeys[which]).astype(LOW)
    one_grad = one_grad + dot_nt(dkey_ref[...], down_w[...])
    if extra:
        across.keep(0)
        feed_own.run("middle_relay")
    for which, (columns, _) in enumerate(groups):
        dvalue_ref[:, columns] = row_total(dvalues[which]).astype(LOW)
    one_grad = one_grad + dot_nt(dvalue_ref[...], at_w[...])
    inputs_part, gain_one = norm_back(x_ref[...].astype(F32), gains_ref[0:1, :], one_grad)
    gain_ref[0:1, :] = gain_one
    dx_ref[...] = (kept_grad[...] + inputs_part).astype(LOW)
    if extra:
        feed_one.run("wait")
        given[0]()
        feed_own.run("end")
        across.keep(1)
        feed_own.run("end_relay")
        feed_one.finish()
        across.finish()
        given[1]()
        feed_own.run("wait")
        feed_own.finish()
    grads.finish()
    sums.finish()
    for scatter in dkeys + dvalues:
        scatter.finish()


def greet_all(far=False):
    rings = [Ring(axis) for axis in ("x", "y", "z")]
    greet(
        *[ring.to_right for ring in rings], *[ring.to_left for ring in rings], sibling(),
        *[ring.to_opposite for ring in rings[1:] if far],
    )


def backward_layer(layer, x, dy, bias, gains, middle, query, key, value, act, attention, feed,
                   operands=()):
    rows, features = x.shape
    hidden = feed[0].shape[1]
    out_shape = (
        jax.ShapeDtypeStruct((rows, features), LOW),
        jax.ShapeDtypeStruct((2, features), F32),
        jax.ShapeDtypeStruct((4, rows, features), LOW),
        jax.ShapeDtypeStruct((4, rows, hidden), LOW),
        jax.ShapeDtypeStruct((rows, features), LOW),
        jax.ShapeDtypeStruct((rows, features), LOW),
        jax.ShapeDtypeStruct((rows, features), LOW),
        jax.ShapeDtypeStruct((rows, features), LOW),
    )
    sums = feed_output(features) * 3 + kept_output(features) if layer == 0 else ()
    return pl.pallas_call(
        functools.partial(backward_kernel, layer, features),
        out_shape=out_shape + sums,
        in_specs=[in_vmem()] * 9 + [anywhere()] * (5 + len(operands)),
        out_specs=[in_vmem()] * len(out_shape) + [anywhere()] * 3 * (len(sums) // 4)
        + [in_vmem()] * (len(sums) // 4),
        scratch_shapes=weight_scratch(features, hidden, 1)
        + scatter_scratch(rows, features) * 3
        + [pltpu.VMEM((rows, features), LOW), pltpu.VMEM((rows, features), F32)]
        + [pltpu.SemaphoreType.DMA((6,))] * 4
        + [pltpu.SemaphoreType.DMA((2, 6))] * 4
        + (
            feed_scratch(features, rows) * 2 + across_scratch(features, rows)
            if layer == 0
            else []
        ),
        compiler_params=pltpu.CompilerParams(
            collective_id=2 + layer, has_side_effects=True, vmem_limit_bytes=62 * 2**20
        ),
        cost_estimate=pl.CostEstimate(
            flops=4 * 10**9, bytes_accessed=24 * 10**6, transcendentals=10**6
        ),
        name=f"layer_backward_{layer}",
    )(x, dy, bias, gains, middle, query, key, value, act, attention, *feed, *operands)


class WeightGather:
    def __init__(self, layer, shard, full, split, sems):
        self.layer, self.full = layer, full
        self.owner = lax.axis_index("section") == layer
        local_sems, pair_sems = sems[0], sems[11:13]
        rings = [tuple(sems[which : which + 2]) for which in (1, 3, 5, 7, 9)]
        x_ring, y_ring, z_ring = Ring("x"), Ring("y"), Ring("z")
        self.y_ring, self.z_ring = y_ring, z_ring
        x_rows, y_rows, y_first, z_first = split
        z_rows = shard.shape[1] - x_rows - y_rows
        z_begin = x_rows + y_rows
        self.with_x = x_rows > 0
        all_x, all_y, all_z = pl.ds(0, x_rows), pl.ds(x_rows, y_rows), pl.ds(z_begin, z_rows)
        self.all_x, self.all_y, self.all_z = all_x, all_y, all_z
        y_half = (pl.ds(x_rows, y_first), pl.ds(x_rows + y_first, y_rows - y_first))
        z_half = (pl.ds(z_begin, z_first), pl.ds(z_begin + z_first, z_rows - z_first))
        me_x, me_y, me_z = x_ring.me, y_ring.me, z_ring.me
        self.pair, self.pair_sems = sibling(), pair_sems

        def local(which):
            src, dst = (
                lambda: (shard.at[me_y, all_y], full.at[me_y, me_x, all_y]),
                lambda: (shard.at[me_z, all_z], full.at[me_z, me_x, all_z]),
                lambda: (shard.at[:, all_x], full.at[:, me_x, all_x]),
            )[which]()
            return pltpu.make_async_copy(src, dst, local_sems.at[which])

        self.local = local
        self.first_y = Gather(
            x_ring,
            lambda block, half: full.at[me_y, block, y_half[half]],
            rings[0],
            lambda half: shard.at[me_y, y_half[half]],
        )
        self.first_z = Gather(
            x_ring,
            lambda block, half: full.at[me_z, block, z_half[half]],
            rings[1],
            lambda half: shard.at[me_z, z_half[half]],
        )
        self.along_x = Gather(
            x_ring,
            lambda block, half: full.at[pl.ds(2 * half, 2), block, all_x],
            rings[2],
            lambda half: shard.at[pl.ds(2 * half, 2), all_x],
        )
        self.along_y = Gather(
            y_ring, lambda block, half: full.at[block, pl.ds(2 * half, 2), all_y], rings[3]
        )
        self.along_z = Gather(
            z_ring, lambda block, half: full.at[block, pl.ds(2 * half, 2), all_z], rings[4]
        )

    def hand(self, which):
        y_ring, z_ring = self.y_ring, self.z_ring
        if which == 2:
            region = (slice(None), slice(None), self.all_x)
        elif which in (0, 3, 5, 7):
            block = {0: y_ring.me, 3: y_ring.left, 5: y_ring.right, 7: y_ring.opposite}[which]
            region = (block, slice(None), self.all_y)
        else:
            block = {1: z_ring.me, 4: z_ring.left, 6: z_ring.right, 8: z_ring.opposite}[which]
            region = (block, slice(None), self.all_z)
        part = self.full.at[region]
        return remote(part, part, self.pair_sems, which, self.pair)

    def handed(self):
        return [which for which in range(9) if which != 2 or self.with_x]

    def start(self):
        self.first_y.start()
        self.first_z.start()
        for which in (0, 1, 2) if self.with_x else (0, 1):
            self.local(which).start()

    def first_relay(self):
        self.first_y.relay()
        self.first_z.relay()
        if self.with_x:
            self.along_x.start()

    def second(self):
        self.first_y.wait_all()
        self.local(0).wait()
        self.along_y.start()
        self.hand(0).start()
        self.first_z.wait_all()
        self.local(1).wait()
        self.along_z.start()
        self.hand(1).start()

    def second_relay(self):
        if self.with_x:
            self.along_x.relay()
        self.along_y.relay()
        self.along_z.relay()

    def last(self):
        if self.with_x:
            self.along_x.wait_all()
            self.local(2).wait()
            self.hand(2).start()
        for which, (gather, wait) in enumerate(
            (gather, wait)
            for wait in ("wait_left", "wait_right", "wait_opposite")
            for gather in (self.along_y, self.along_z)
        ):
            getattr(gather, wait)()
            self.hand(3 + which).start()

    def finish(self):
        for which in self.handed():
            self.hand(which).wait_send()
        for gather in (self.first_y, self.first_z, self.along_y, self.along_z):
            gather.finish()
        if self.with_x:
            self.along_x.finish()

    def receive(self):
        for which in self.handed():
            self.hand(which).wait_recv()

    def steps(self, *names):
        @pl.when(self.owner)
        def _():
            for name in names:
                getattr(self, name)()

    def end(self):
        self.steps("last", "finish")

        @pl.when(jnp.logical_not(self.owner))
        def _():
            self.receive()


def weight_sems():
    dma = pltpu.SemaphoreType.DMA
    return [dma((3,))] + [dma((6,))] * 10 + [dma((9,))] * 2


def weights_kernel(shard_ref, gain_ref, full_ref, gain_mine, gain_theirs, *sems):
    gain_local, gain_send, gain_recv = sems[13:]
    weights = WeightGather(0, shard_ref, full_ref, (96, 96, 48, 48), sems[:13])
    x_ring = Ring("x")
    mine_x, pair = x_ring.me, sibling()
    greet_all()

    def gain_copy(which, block, src=None):
        part = gain_mine.at[block]
        target = x_ring.to_left if which == 1 else x_ring.to_right
        return remote(part if src is None else src, part, (gain_send, gain_recv), which, target)

    gain_keep = pltpu.make_async_copy(gain_ref, gain_mine.at[mine_x], gain_local.at[0])
    weights.steps("start")
    gain_keep.start()
    gain_copy(0, mine_x, gain_ref).start()
    gain_copy(1, mine_x, gain_ref).start()
    weights.steps("first_relay")
    gain_copy(0, x_ring.left).wait_recv()
    gain_copy(2, x_ring.left).start()
    weights.steps("second")
    gain_copy(1, x_ring.right).wait_recv()
    gain_copy(2, x_ring.opposite).wait_recv()
    gain_keep.wait()
    gains = remote(gain_mine, gain_theirs, (gain_send, gain_recv), 3, pair)
    gains.start()
    weights.steps("second_relay")
    weights.end()
    gains.wait()
    for which in range(3):
        gain_copy(which, mine_x).wait_send()


def gather_weights(shard, gain):
    mats, share, features = shard.shape
    gains = jax.ShapeDtypeStruct((4,) + gain.shape, LOW)
    dma = pltpu.SemaphoreType.DMA
    return pl.pallas_call(
        weights_kernel,
        out_shape=(jax.ShapeDtypeStruct((mats, 4, share, features), LOW), gains, gains),
        in_specs=[anywhere()] * 2,
        out_specs=[anywhere()] * 3,
        scratch_shapes=weight_sems() + [dma((1,)), dma((4,)), dma((4,))],
        compiler_params=pltpu.CompilerParams(collective_id=4, has_side_effects=True),
        cost_estimate=pl.CostEstimate(flops=0, bytes_accessed=30 * 10**6, transcendentals=0),
        name="gather_weights",
    )(shard, gain)


class SmallSum:
    def __init__(self, ring, slots, sems):
        self.ring, self.slots, self.sems = ring, slots, sems

    def copy(self, which, block):
        target = self.ring.to_left if which == 1 else self.ring.to_right
        part = self.slots.at[block]
        return remote(part, part, self.sems, which, target)

    def start(self):
        self.copy(0, self.ring.me).start()
        self.copy(1, self.ring.me).start()

    def relay(self):
        self.copy(0, self.ring.left).wait_recv()
        self.copy(2, self.ring.left).start()

    def result(self):
        self.copy(1, self.ring.right).wait_recv()
        self.copy(2, self.ring.opposite).wait_recv()
        return (self.slots[0] + self.slots[1]) + (self.slots[2] + self.slots[3])

    def finish(self):
        for which in range(3):
            self.copy(which, self.ring.me).wait_send()


class PlaneSum:
    def __init__(self, near, far, source, out, size, first, scratch, sems, keep, direct=False,
                 base=0):
        if direct:
            self.arrived, self.mid, self.done = scratch
        else:
            self.landing, self.passing, self.arrived, self.mid, self.done = scratch
        self.direct, self.base = direct, base
        self.out, self.size, self.near, self.far, self.keep = out, size, near, far, keep
        self.halves = ((0, first), (first, size - first))

        def rows(block, half):
            begin, count = (0, size) if half is None else self.halves[half]
            return pl.ds(pl.multiple_of(base + block * size + begin, 16), count)

        def half_rows(half):
            return pl.ds(0, size) if half is None else pl.ds(*self.halves[half])

        self.half_rows = half_rows
        def part(block, half):
            return source.at[rows(block, half)]

        if direct:
            self.scatter = DirectScatter(near, part, lambda side: self.arrived.at[side], sems[0])
        else:
            self.scatter = Scatter(
                near,
                part,
                lambda half: self.landing.at[half_rows(half)],
                lambda half: self.passing.at[half_rows(half)],
                lambda side, half: self.arrived.at[side, half_rows(half)],
                sems[0],
            )
        kind = DirectGather if direct else Gather
        self.gather = kind(far, lambda block, half: self.mid.at[block, half_rows(half)], sems[1])
        self.spread = kind(
            near,
            lambda block, half: out.at[rows(block, half)],
            sems[2],
            lambda half: self.done.at[half_rows(half)],
        )

    def start(self):
        self.scatter.start_far()
        self.scatter.start_near()

    def relay(self):
        self.scatter.relay()

    def middle(self):
        self.scatter.wait()
        if self.direct:
            self.mid[self.far.me] = self.scatter.whole().astype(LOW)
        else:
            for half in range(2):
                self.mid[self.far.me, self.half_rows(half)] = self.scatter.total(half).astype(LOW)
        self.gather.start()

    def middle_relay(self):
        self.gather.relay()

    def own(self):
        place = pl.ds(
            pl.multiple_of(self.base + self.near.me * self.size, 16), self.size
        )
        return pltpu.make_async_copy(self.done, self.out.at[place], self.keep)

    def end(self):
        self.gather.wait_all()
        four = [self.mid[block].astype(F32) for block in range(4)]
        self.done[...] = ((four[0] + four[1]) + (four[2] + four[3])).astype(LOW)
        self.spread.start()
        self.own().start()

    def end_relay(self):
        self.spread.relay()

    def wait(self):
        self.spread.wait_all()
        self.own().wait()

    def finish(self):
        self.scatter.finish()
        self.gather.finish()
        self.spread.finish()


FEED_BLOCK, AT_BLOCK = 144, 80


def feed_output(features):
    return (jax.ShapeDtypeStruct((2, 4 * FEED_BLOCK, features), LOW),)


def kept_output(features):
    return (jax.ShapeDtypeStruct((2, 4 * AT_BLOCK, features), LOW),)


def plane_scratch(size, features, direct=False):
    dma = pltpu.SemaphoreType.DMA

    def low(*shape):
        return pltpu.VMEM(shape + (features,), LOW)

    if direct:
        return [low(3, size), low(4, size), low(size)] + [dma((3,))] * 6
    return [low(size), low(size), low(2, size), low(4, size), low(size)] + [dma((6,))] * 6


def feed_scratch(features, rows):
    dma = pltpu.SemaphoreType.DMA
    return (
        [pltpu.VMEM((2, 2, 4, rows, features), LOW), pltpu.VMEM((2, 4 * FEED_BLOCK, features), LOW)]
        + plane_scratch(FEED_BLOCK, features) * 2
        + [dma((2,)), dma((2,)), dma((2,)), dma((2,)), dma((1,)), dma((1,))]
    )


def across_scratch(features, rows):
    share = features // 4
    dma = pltpu.SemaphoreType.DMA

    def low(*shape):
        return pltpu.VMEM(shape + (features,), LOW)

    return (
        [low(2, 2, rows), low(2, 2, rows), low(2, features)]
        + ([low(share), low(share), low(2, share)] + [dma((6,))] * 2) * 2
        + [dma((4,)), dma((4,)), dma((4,))]
    )


WIDE_PIECES = ((0, 0, 80, 48, 0), (1, 0, 80, 48, 1))
FINE_PIECES = ((0, 0, 48, 32, 0), (0, 192, 32, 16, 1), (1, 0, 48, 32, 1), (1, 192, 32, 16, 0))


def attention_scratch(features, pieces, direct):
    dma = pltpu.SemaphoreType.DMA
    scratch = []
    for piece in pieces:
        scratch += plane_scratch(piece[2], features, direct)
    return scratch + [dma((len(pieces),)), dma((2,)), dma((2,))]


def take_planes(take, count, direct=False):
    planes = []
    for _ in range(count):
        scratch = [next(take) for _ in range(3 if direct else 5)]
        sems = [next(take) for _ in range(6)]
        planes.append((scratch, [tuple(sems[i : i + 2]) for i in (0, 2, 4)]))
    return planes


def hand_over(layer, src, dst, sems, which=0):
    section = lax.axis_index("section")
    copy = functools.partial(remote, src, dst, sems, which, sibling())

    def start():
        @pl.when(section != layer)
        def _():
            copy().start()

    def wait():
        @pl.when(section != layer)
        def _():
            copy().wait_send()

        @pl.when(section == layer)
        def _():
            copy().wait_recv()

    return start, wait


class SwappedInputs:
    def __init__(self, zero, other, targets, local_sems, swap):
        self.zero, self.other, self.targets = zero, other, targets
        self.local_sems, self.swap, self.pair = local_sems, swap, sibling()

    def copies(self, first, which):
        own, sent = (self.zero, self.other) if first else (self.other, self.zero)
        target = self.targets[which]
        return (
            lambda: pltpu.make_async_copy(own[which], target.at[0], self.local_sems.at[which]),
            lambda: remote(sent[which], target.at[1], self.swap, which, self.pair),
        )

    def start(self):
        section = lax.axis_index("section")
        for first in (True, False):

            @pl.when(section == (0 if first else 1))
            def _(first=first):
                for which in range(len(self.targets)):
                    self.copies(first, which)[1]().start()
                for which in range(len(self.targets)):
                    self.copies(first, which)[0]().start()

    def wait(self, whiches):
        for which in whiches:
            keep, send = self.copies(True, which)
            keep().wait()
            send().wait_recv()

    def finish(self):
        for which in range(len(self.targets)):
            self.copies(True, which)[1]().wait_send()


class AttentionSum:
    def __init__(self, layer, kept, results, take, pieces, direct):
        out, other = results
        planes = take_planes(take, len(pieces), direct)
        keep, send, recv = [next(take) for _ in range(3)]
        y_ring, z_ring = Ring("y"), Ring("z")
        orders = ((y_ring, z_ring), (z_ring, y_ring))
        self.pieces = pieces
        self.planes = [
            PlaneSum(
                *orders[order], kept.at[matrix], out.at[matrix], size, first, *planes[which],
                keep.at[which], direct, base,
            )
            for which, (matrix, base, size, first, order) in enumerate(pieces)
        ]
        self.given = [
            hand_over(layer, out.at[which], other.at[which], (send, recv), which)
            for which in range(2)
        ]

    def run(self, name, matrix=None):
        for plane, piece in zip(self.planes, self.pieces):
            if matrix is None or piece[0] == matrix:
                getattr(plane, name)()

    def hand(self, matrix):
        self.run("wait", matrix)
        self.given[matrix][0]()

    def finish(self):
        self.run("finish")
        for given in self.given:
            given[1]()


class FeedSum:
    def __init__(self, features, operands, out, take):
        two, pre, hidden, out_all = operands
        self.features = features
        self.feed_in, self.feed_sum = next(take), next(take)
        planes = take_planes(take, 2)
        local_sems, swap_send, swap_recv, keep, end_send, end_recv = [
            next(take) for _ in range(6)
        ]
        self.end_sems = (end_send, end_recv)
        self.inputs = SwappedInputs(
            (two, pre), (hidden, out_all), (self.feed_in.at[0], self.feed_in.at[1]), local_sems,
            (swap_send, swap_recv),
        )
        y_ring, z_ring = Ring("y"), Ring("z")
        orders = ((y_ring, z_ring), (z_ring, y_ring))
        self.planes = [
            PlaneSum(
                *orders[which], self.feed_sum.at[which], out.at[which], FEED_BLOCK, 80,
                *planes[which], keep.at[which],
            )
            for which in range(2)
        ]

    def products(self):
        self.inputs.wait((0, 1))
        features, whole = self.features, 4 * FEED_BLOCK
        right = self.feed_in[1].reshape(-1, features)
        for begin in range(0, features, 256):
            count = min(256, features - begin)
            left = self.feed_in[0, :, :, :, pl.ds(begin, count)].reshape(-1, count)
            product = dot_tn(left, right).astype(LOW)
            first = max(0, min(count, whole - begin))
            if first:
                self.feed_sum[0, pl.ds(begin, first)] = product[:first]
            if first < count:
                self.feed_sum[1, pl.ds(begin + first - whole, count - first)] = product[first:]
        spare = 2 * whole - features
        self.feed_sum[1, pl.ds(whole - spare, spare)] = jnp.zeros((spare, features), LOW)
        self.run("start")

    def run(self, name):
        for plane in self.planes:
            getattr(plane, name)()

    def finish(self):
        self.inputs.finish()
        self.run("finish")


class AcrossSum:
    def __init__(self, features, operands, kept, take):
        one, mixed, dq, dk, dv, branch = operands
        self.features, self.share, self.kept = features, features // 4, kept
        share = self.share
        self.at_left, self.at_right, self.at_sum = [next(take) for _ in range(3)]
        self.halves = halves = ((0, 144), (144, share - 144))
        x_ring = Ring("x")
        self.across = []
        for which in range(2):
            landing, passing, arrived, send, recv = [next(take) for _ in range(5)]

            def part(block, half, which=which):
                begin, count = halves[half]
                row = pl.multiple_of(block * share + begin, 16)
                return self.at_sum.at[which, pl.ds(row, count)]

            def cut(ref):
                return lambda half: ref.at[pl.ds(*halves[half])]

            self.across.append(
                Scatter(
                    x_ring, part, cut(landing), cut(passing),
                    lambda side, half, arrived=arrived: arrived.at[side, pl.ds(*halves[half])],
                    (send, recv),
                )
            )
        local_sems, swap_send, swap_recv = [next(take) for _ in range(3)]
        self.inputs = SwappedInputs(
            (one, dq, one, dk),
            (one, dv, mixed, branch),
            (self.at_left.at[0], self.at_right.at[0], self.at_left.at[1], self.at_right.at[1]),
            local_sems,
            (swap_send, swap_recv),
        )

    def products(self, which):
        self.inputs.wait((2 * which, 2 * which + 1))
        features = self.features
        right = self.at_right[which].reshape(-1, features)
        for begin in range(0, features, 256):
            count = min(256, features - begin)
            left = self.at_left[which, :, :, pl.ds(begin, count)].reshape(-1, count)
            self.at_sum[which, pl.ds(begin, count)] = dot_tn(left, right).astype(LOW)
        self.across[which].start_far()

    def relay(self, which):
        self.across[which].relay()
        self.across[which].start_near()

    def keep(self, which):
        across = self.across[which]
        across.wait()
        for half in range(2):
            self.kept[which, pl.ds(*self.halves[half])] = across.total(half).astype(LOW)
        spare = 4 * AT_BLOCK - self.share
        self.kept[which, pl.ds(self.share, spare)] = jnp.zeros((spare, self.features), LOW)

    def finish(self):
        self.inputs.finish()
        for across in self.across:
            across.finish()


def gradient_kernel(features, *refs):
    take = iter(refs)

    def some(count):
        return [next(take) for _ in range(count)]

    operands = some(6)
    y_a, y_b, dx_a, dx_b, feed_zero, gain_in, kept_one = some(7)
    (feed_given,), at_zero, at_one = some(1), some(2), some(2)
    act_out, grad_out, gain_out = some(3)
    (kept_zero,) = some(1)
    sums = AcrossSum(features, operands, kept_zero, take)
    zero = AttentionSum(0, kept_zero, at_zero, take, FINE_PIECES, True)
    one = AttentionSum(1, kept_one, at_one, take, WIDE_PIECES, False)
    (gain_pair, gain_x, gain_y, gain_z, gain_send, gain_recv, last_send, last_recv, keep_sems,
     feed_send, feed_recv) = some(11)
    x_ring, y_ring, z_ring = Ring("x"), Ring("y"), Ring("z")
    pair, section = sibling(), lax.axis_index("section")
    greet_all(far=True)
    sums.inputs.start()
    feed = hand_over(0, feed_zero, feed_given, (feed_send, feed_recv))

    def last_copies(y, dx):
        return (
            remote(y, act_out.at[section], (last_send, last_recv), 0, pair),
            remote(dx, grad_out.at[section], (last_send, last_recv), 1, pair),
        )

    def keep_copies(y, dx):
        return (
            pltpu.make_async_copy(y, act_out.at[section], keep_sems.at[0]),
            pltpu.make_async_copy(dx, grad_out.at[section], keep_sems.at[1]),
        )

    @pl.when(section == 0)
    def _():
        for copy in last_copies(y_b, dx_b) + keep_copies(y_a, dx_a):
            copy.start()

    @pl.when(section == 1)
    def _():
        for copy in last_copies(y_a, dx_a) + keep_copies(y_b, dx_b):
            copy.start()

    gain_pair[0] = gain_in[...]
    swap_gain = remote(gain_pair.at[0], gain_pair.at[1], (gain_send, gain_recv), 9, pair)
    swap_gain.start()
    one.run("start")
    sums.products(0)
    sums.products(1)
    feed[0]()
    swap_gain.wait()
    gain_x[x_ring.me] = gain_pair[0] + gain_pair[1]
    small = [
        SmallSum(ring, slots, (gain_send.at[pl.ds(3 * i, 3)], gain_recv.at[pl.ds(3 * i, 3)]))
        for i, (ring, slots) in enumerate(((x_ring, gain_x), (y_ring, gain_y), (z_ring, gain_z)))
    ]
    small[0].start()
    one.run("relay")
    sums.relay(0)
    small[0].relay()
    one.run("middle")
    gain_y[y_ring.me] = small[0].result()
    small[1].start()
    one.run("middle_relay")
    small[1].relay()
    sums.keep(0)
    sums.relay(1)
    zero.run("start", 0)
    one.run("end")
    gain_z[z_ring.me] = small[1].result()
    small[2].start()
    zero.run("middle", 0)
    one.run("end_relay")
    small[2].relay()
    zero.run("end", 0)
    gain_out[...] = small[2].result()
    sums.keep(1)
    zero.run("start", 1)
    one.hand(0)
    one.hand(1)
    zero.hand(0)
    zero.run("middle", 1)
    zero.run("end", 1)
    zero.hand(1)
    zero.finish()
    one.finish()
    sums.finish()
    feed[1]()
    for each in small:
        each.finish()
    for copy in last_copies(y_a, dx_a) + keep_copies(y_a, dx_a):
        copy.wait()


def sum_gradients(features, rows, operands, last, gain, kept):
    dma = pltpu.SemaphoreType.DMA
    small = [pltpu.VMEM((4, 8, features), F32)] * 3
    return pl.pallas_call(
        functools.partial(gradient_kernel, features),
        out_shape=feed_output(features)
        + kept_output(features) * 4
        + (
            jax.ShapeDtypeStruct((2, rows, features), LOW),
            jax.ShapeDtypeStruct((2, rows, features), LOW),
            jax.ShapeDtypeStruct((8, features), F32),
        ),
        in_specs=[anywhere()] * 11 + [in_vmem()] * 2,
        out_specs=[anywhere()] * 7 + [in_vmem()],
        scratch_shapes=[pltpu.VMEM((2, 4 * AT_BLOCK, features), LOW)]
        + across_scratch(features, rows)
        + attention_scratch(features, FINE_PIECES, True)
        + attention_scratch(features, WIDE_PIECES, False)
        + [pltpu.VMEM((2, 8, features), F32)]
        + small
        + [dma((10,)), dma((10,)), dma((2,)), dma((2,)), dma((2,)), dma((1,)), dma((1,))],
        compiler_params=pltpu.CompilerParams(
            collective_id=5, has_side_effects=True, vmem_limit_bytes=60 * 2**20
        ),
        cost_estimate=pl.CostEstimate(
            flops=3 * 10**9, bytes_accessed=60 * 10**6, transcendentals=0
        ),
        name="sum_gradients",
    )(*operands, *last, gain, kept)


def doc_numbers(lengths, positions):
    doc_ends = jnp.cumsum(lengths)
    return jnp.sum((positions[:, None] >= doc_ends[None, :]).astype(jnp.int32), axis=1)


def swapped(block):
    return lax.ppermute(block, "section", [(0, 1), (1, 0)])


def body(tokens, cotangent, doc_lengths, norm_gains, w_qkv, w_out, w_up, w_down):
    batches, rows, features = tokens.shape
    share = w_qkv.shape[1]
    seq_rows = rows * lax.axis_size("tensor")
    section = lax.axis_index("section")
    is_first = section == 0

    def choose(zero_side, one_side):
        return jnp.where(is_first, zero_side, one_side)

    own_tokens = lax.dynamic_index_in_dim(tokens, section, 0, keepdims=False)
    own_cotangent = lax.dynamic_index_in_dim(cotangent, section, 0, keepdims=False)
    lengths = lax.dynamic_index_in_dim(doc_lengths, section, 0, keepdims=False)
    own_places = lax.axis_index("tensor") * rows + jnp.arange(rows, dtype=jnp.int32)
    all_places = jnp.arange(seq_rows, dtype=jnp.int32)
    own_docs = doc_numbers(lengths, own_places)
    all_docs = doc_numbers(lengths, all_places)
    allowed = (all_places[None, :] <= own_places[:, None]) & (
        all_docs[None, :] == own_docs[:, None]
    )
    bias = jnp.where(allowed, 0.0, -1e30).astype(F32)
    bias_turned = bias.T

    feed = (w_up[0], swapped(w_up[0]), w_down[0], swapped(w_down[0]))
    shard = jnp.stack(
        [w_qkv[0, :, :features], w_qkv[0, :, features : 2 * features], w_qkv[0, :, 2 * features :],
         w_out[0]]
    )
    gain_shard = jnp.pad(norm_gains[0], ((0, 14), (0, 0)))
    at_zero, gain_mine, gain_theirs = gather_weights(shard, gain_shard)
    attention = [at_zero.reshape(4, features, features), None]

    def whole_gains(block):
        return block[:, :2].transpose(1, 0, 2).reshape(2, features).astype(F32)

    gain_mine, gain_theirs = whole_gains(gain_mine), whole_gains(gain_theirs)
    gains = (choose(gain_mine, gain_theirs), choose(gain_theirs, gain_mine))

    inputs = own_tokens
    saved = []
    for layer in range(2):
        results = forward_layer(
            layer, inputs, bias, gains[layer], attention[layer], feed,
            (shard,) if layer == 0 else (),
        )
        if layer == 0:
            attention[1] = results[10].reshape(4, features, features)
        saved.append((inputs,) + tuple(results[:10]))
        inputs = results[0]

    grad = own_cotangent
    gain_grads, input_grads, operands = [None, None], [None, None], ()
    for layer in (1, 0):
        (x, _, middle, normed_one, query, key, value, mixed, normed_two, act, hidden) = saved[layer]
        results = backward_layer(
            layer, x, grad, bias_turned, gains[layer], middle, query, key, value, act,
            attention[layer], feed, operands + (saved[0][8], saved[0][10]) if layer == 0 else (),
        )
        (grad, gain_grads[layer], out_all, pre_grad, branch, dquery, dkey, dvalue) = results[:8]
        input_grads[layer] = grad
        operands = (
            normed_two, pre_grad, hidden, out_all, normed_one, mixed, dquery, dkey, dvalue, branch,
        )
    feed_one, feed_one_given, feed_zero, kept_one = results[8:]
    gain_rows = jnp.concatenate(gain_grads + [jnp.zeros((4, features), F32)], axis=0)
    (feed_zero_given, at_zero, at_zero_given, at_one, at_one_given, activations, input_grads,
     gain_total) = sum_gradients(
        features, rows, operands[4:], (saved[0][1], saved[1][1], *input_grads, feed_zero),
        gain_rows, kept_one,
    )
    gain_own = lax.dynamic_slice(
        gain_total, (2 * section, lax.axis_index("tensor") * share), (2, share)
    )

    def whole(block):
        return block.reshape(-1, features)[:features].astype(F32)[None]

    first_half = choose(at_zero, at_one_given)[:, :share].astype(F32)
    other_half = choose(at_zero_given, at_one)[:, :share].astype(F32)
    grad_qkv = jnp.concatenate([first_half[0], first_half[1], other_half[0]], axis=1)
    return (
        activations[None],
        input_grads[None],
        gain_own[None],
        grad_qkv[None],
        other_half[1][None],
        whole(choose(feed_zero, feed_one_given)),
        whole(choose(feed_zero_given, feed_one)),
    )


def solution(mesh):
    placed = (
        P("dp", "tensor", None),
        P("dp", "tensor", None),
        P("dp", None),
        P("section", None, "tensor"),
        P("section", "tensor", None),
        P("section", "tensor", None),
        P("section", None, "tensor"),
        P("section", "tensor", None),
    )
    return jax.shard_map(
        body,
        mesh=mesh,
        in_specs=placed,
        out_specs=(
            P("section", "dp", "tensor", None),
            P("section", "dp", "tensor", None),
            P("section", None, "tensor"),
            P("section", "tensor", None),
            P("section", "tensor", None),
            P("section", None, "tensor"),
            P("section", "tensor", None),
        ),
        check_vma=False,
    )
```

profile of v0, /device:TPU:0, one launch (start us, length us, event | category | flops | bytes accessed | tf_op | source)
XLA Modules:
  0.0 448.2 jit_solution(9009546426192763570)
XLA Ops:
  0.6 0.0 copy-start
  0.6 0.0 copy-start.9
  0.7 0.1 collective-permute-start
  0.8 0.5 collective-permute-start.1
  1.2 0.1 copy-done
  1.3 0.2 reduce-window.8
  1.5 1.3 pad.4.gain_ref
  2.8 1.8 fusion.12
  4.6 0.0 copy-done.9
  4.6 1.9 pad_maximum_fusion.shard_ref.refs_8_
  6.5 0.0 copy-start.12
  6.5 0.0 copy-start.13
  6.5 68.0 %gather_weights.1 = (bf16[4,4,272,1088]{3,2,1,0:T(8,128)(2,1)}, bf16[4,16,272]{2,1,0:T(8,128)(2,1)}, bf16[4,16,272]{2,1,0:T(8,128)(2,1)}) custom-call(bf16[4,272,1088]{2,1,0:T(8,128)(2,1)} %pad_maximum_fusion.shard_ref.refs_8_, bf16[16,272]{1,0:T(8,128)(2,1)} %pad.4.gain_ref), custom_call_target="tpu_custom_call" | custom-call | bytes 30000000 | tf_op jit(solution)/shard_map/gather_weights/pallas_call | solution.py:943
  74.5 0.8 fusion.9
  75.3 0.7 select_n.68.refs_2_.refs_3_
  76.0 0.7 select_n.72.refs_2_.refs_3_
  76.7 0.1 pad.7.clone
  76.8 0.1 convert_reduce_fusion
  76.9 0.1 convert_reduce_fusion.1
  77.0 0.8 fusion.7.refs_1_
  77.7 0.8 fusion.5.refs_2_
  78.5 0.0 copy-done.12
  78.5 0.0 copy-done.13
  78.5 0.8 dynamic-slice_bitcast_fusion
  79.3 0.0 collective-permute-done.refs_5_.refs_11_
  79.3 0.0 collective-permute-done.1.refs_7_.refs_13_
  79.3 68.8 %layer_forward_0.1 = (bf16[96,1088]{1,0:T(8,128)(2,1)}, f32[96,1088]{1,0:T(8,128)}, bf16[96,1088]{1,0:T(8,128)(2,1)}, bf16[96,1088]{1,0:T(8,128)(2,1)}, bf16[4,9...) custom-call(bf16[96,1088]{1,0:T(8,128)(2,1)} %get-tuple-element.117., ...), custom_call_target="tpu_custom_call" | custom-call | flops 3000000000 | bytes 24000000 | tf_op jit(solution)/shard_map/layer_forward_0/pallas_call | solution.py:513
  148.1 48.7 %layer_forward_1.1 = (bf16[96,1088]{1,0:T(8,128)(2,1)}, f32[96,1088]{1,0:T(8,128)}, bf16[96,1088]{1,0:T(8,128)(2,1)}, bf16[96,1088]{1,0:T(8,128)(2,1)}, bf16[4,9...) custom-call(bf16[96,1088]{1,0:T(8,128)(2,1)} %get-tuple-element.62.r, ...), custom_call_target="tpu_custom_call" | custom-call | flops 3000000000 | bytes 24000000 | tf_op jit(solution)/shard_map/layer_forward_1/pallas_call | solution.py:513
  196.8 47.3 %layer_backward_1.1 = (bf16[96,1088]{1,0:T(8,128)(2,1)}, f32[2,1088]{1,0:T(2,128)}, bf16[4,96,1088]{2,1,0:T(8,128)(2,1)}, bf16[4,96,1088]{2,1,0:T(8,128)(2,1)}, ...) custom-call(bf16[96,1088]{1,0:T(8,128)(2,1)} %get-tuple-element.62.ref, ...), custom_call_target="tpu_custom_call" | custom-call | flops 4000000000 | bytes 24000000 | tf_op jit(solution)/shard_map/layer_backward_1/pallas_call | solution.py:739
  244.1 0.0 copy-start.14
  244.2 96.8 %layer_backward_0.1 = (bf16[96,1088]{1,0:T(8,128)(2,1)}, f32[2,1088]{1,0:T(2,128)}, bf16[4,96,1088]{2,1,0:T(8,128)(2,1)}, bf16[4,96,1088]{2,1,0:T(8,128)(2,1)}, ...) custom-call(bf16[96,1088]{1,0:T(8,128)(2,1)} %get-tuple-element.117., ...), custom_call_target="tpu_custom_call" | custom-call | flops 4000000000 | bytes 24000000 | tf_op jit(solution)/shard_map/layer_backward_0/pallas_call | solution.py:739
  340.9 0.0 copy-done.14
  340.9 1.4 maximum_maximum_fusion.refs_11_
  342.3 0.0 copy-start.4
  342.3 84.5 %sum_gradients.1 = (bf16[2,576,1088]{2,1,0:T(8,128)(2,1)}, bf16[2,320,1088]{2,1,0:T(8,128)(2,1)}, bf16[2,320,1088]{2,1,0:T(8,128)(2,1)}, bf16[2,320,1088]{2,1,0:...) custom-call(bf16[96,1088]{1,0:T(8,128)(2,1)} %get-tuple-element.60.r, ...), custom_call_target="tpu_custom_call" | custom-call | flops 3000000000 | bytes 60000000 | tf_op jit(solution)/shard_map/sum_gradients/pallas_call | solution.py:1438
  426.8 0.0 copy-done.4
  426.8 2.3 broadcast_select_fusion
  429.1 0.0 copy-start.2
  429.1 0.0 copy-start.3
  429.1 2.9 fusion
  432.0 0.0 copy-done.2
  432.0 1.5 copy-done.3
  433.5 0.3 broadcast_select_fusion.1
  433.8 0.0 copy-start.7
  433.8 0.0 copy-start.8
  433.8 2.6 fusion.1
  436.4 0.0 copy-done.7
  436.4 0.5 copy-done.8
  436.9 0.2 fusion.2
  437.1 0.0 copy-start.5
  437.1 0.0 copy-start.6
  437.1 1.2 fusion.11
  438.3 0.6 copy-done.5
  438.9 0.4 copy-done.6
  439.4 0.2 fusion.3
  439.5 1.2 slice_bitcast_fusion.3
  440.7 0.0 copy-start.11
  440.7 4.2 concatenate.7
  444.9 1.4 dynamic-slice_bitcast_fusion.2
  446.3 0.0 copy-done.11
  446.3 0.8 copy.21
  447.0 0.0 copy-done.10
  447.1 0.8 copy.22
  447.8 0.0 copy-done.1
  (7 shorter events, 0.0 us)
Async XLA Ops:
  0.6 0.7 copy-start
  0.6 3.9 copy-start.9
  0.7 78.7 %collective-permute-start = (bf16[1088,1088]{1,0:T(8,128)(2,1)}, bf16[1088,1088]{1,0:T(8,128)(2,1)}, u32[]{:S(2)}, u32[]{:S(2)}) collective-permute-start(bf16[1088,1088]{1,0:T(8,128)(2,1)} %bitcast.43), channel_id=1, source_target_pairs={{0,64},{64,0},{1,65},{65,1},{2,66},{66,2},{3,67},{67,3},{4,68},{68... | collective-permute-start | bytes 7102472 | tf_op jit(solution)/shard_map/ppermute | solution.py:1472
  0.8 78.6 %collective-permute-start.1 = (bf16[1088,1088]{1,0:T(8,128)(2,1)}, bf16[1088,1088]{1,0:T(8,128)(2,1)}, u32[]{:S(2)}, u32[]{:S(2)}) collective-permute-start(bf16[1088,1088]{1,0:T(8,128)(2,1)} %bitcast.48), channel_id=1, source_target_pairs={{0,64},{64,0},{1,65},{65,1},{2,66},{66,2},{3,67},{67,3},{4,68},{68... | collective-permute-start | bytes 7102472 | tf_op jit(solution)/shard_map/ppermute | solution.py:1472
  6.5 72.0 %copy-start.12 = (bf16[2,96,1088]{2,1,0:T(8,128)(2,1)S(1)}, bf16[2,96,1088]{2,1,0:T(8,128)(2,1)}, u32[]{:S(2)}) copy-start(bf16[2,96,1088]{2,1,0:T(8,128)(2,1)} %param.9) | copy-start | bytes 1253380
  6.5 72.0 %copy-start.13 = (bf16[2,96,1088]{2,1,0:T(8,128)(2,1)S(1)}, bf16[2,96,1088]{2,1,0:T(8,128)(2,1)}, u32[]{:S(2)}) copy-start(bf16[2,96,1088]{2,1,0:T(8,128)(2,1)} %param.8) | copy-start | bytes 1253380
  244.1 96.8 %copy-start.14 = (f32[2,1088]{1,0:T(2,128)S(1)}, f32[2,1088]{1,0:T(2,128)}, u32[]{:S(2)}) copy-start(f32[2,1088]{1,0:T(2,128)} %get-tuple-element.95) | copy-start | bytes 26116
  342.3 84.5 %copy-start.4 = (bf16[2,576,1088]{2,1,0:T(8,128)(2,1)S(1)}, bf16[2,576,1088]{2,1,0:T(8,128)(2,1)}, u32[]{:S(2)}) copy-start(bf16[2,576,1088]{2,1,0:T(8,128)(2,1)} %get-tuple-element.106) | copy-start | bytes 7520260
  429.1 2.9 copy-start.2
  429.1 4.4 copy-start.3
  433.8 2.7 copy-start.7
  433.8 3.1 copy-start.8
  437.1 1.8 copy-start.5
  437.1 2.3 copy-start.6
  440.7 5.5 %copy-start.11 = (bf16[2,96,1088]{2,1,0:T(8,128)(2,1)S(1)}, bf16[2,96,1088]{2,1,0:T(8,128)(2,1)}, u32[]{:S(2)}) copy-start(bf16[2,96,1088]{2,1,0:T(8,128)(2,1)} %get-tuple-element.97) | copy-start | bytes 1253380
  440.7 6.3 %copy-start.10 = (bf16[2,96,1088]{2,1,0:T(8,128)(2,1)S(1)}, bf16[2,96,1088]{2,1,0:T(8,128)(2,1)}, u32[]{:S(2)}) copy-start(bf16[2,96,1088]{2,1,0:T(8,128)(2,1)} %get-tuple-element.98) | copy-start | bytes 1253380
  440.7 7.1 %copy-start.1 = (s32[2,4]{1,0:T(2,128)S(1)}, s32[2,4]{1,0:T(2,128)}, u32[]{:S(2)}) copy-start(s32[2,4]{1,0:T(2,128)} %param.10) | copy-start | bytes 100
where the time goes:
time: 457 us; the launch traced here: 448 us
  Pallas kernels  414 us (91%)
  local copies, waits for them, and re-layouts  17.9 us (4%)
  other arithmetic  14.4 us (3%)
    pallas_call x2, Pallas kernels, backward_layer(): pl.pallas_call(functools.partial(backward_kernel, layer, features), out_s...  144 us
    pallas_call x2, Pallas kernels, forward_layer(): pl.pallas_call(functools.partial(forward_kernel, layer, features), out_sh...  117 us
    pallas_call x1, Pallas kernels, sum_gradients(): pl.pallas_call(functools.partial(gradient_kernel, features), out_shape=fe...  84.5 us
    pallas_call x1, Pallas kernels, gather_weights(): pl.pallas_call(weights_kernel, out_shape=(jax.ShapeDtypeStruct((mats, 4,...  68 us
  transfers between devices with their start and end apart: 2, of which 0 were waited for; matrix products, arithmetic and copies ran while one was open for 2% of the time, Pallas kernels for 15%

commit v1 on v0

--- a/solution.py
+++ b/solution.py
@@ -513,7 +513,7 @@
     return pl.pallas_call(
         functools.partial(forward_kernel, layer, features),
         out_shape=out_shape + following,
-        in_specs=[in_vmem()] * 3 + [anywhere()] * (5 + len(shard)),
+        in_specs=[in_vmem()] * 3 + [anywhere()] * 5 + [in_vmem()] * len(shard),
         out_specs=[in_vmem()] * len(out_shape) + [anywhere()] * len(following),
         scratch_shapes=weight_scratch(features, hidden)
         + scatter_scratch(rows, features)
@@ -905,7 +905,7 @@
 
 def weights_kernel(shard_ref, gain_ref, full_ref, gain_mine, gain_theirs, *sems):
     gain_local, gain_send, gain_recv = sems[13:]
-    weights = WeightGather(0, shard_ref, full_ref, (96, 96, 48, 48), sems[:13])
+    weights = WeightGather(0, shard_ref, full_ref, (64, 112, 64, 48), sems[:13])
     x_ring = Ring("x")
     mine_x, pair = x_ring.me, sibling()
     greet_all()
@@ -943,7 +943,7 @@
     return pl.pallas_call(
         weights_kernel,
         out_shape=(jax.ShapeDtypeStruct((mats, 4, share, features), LOW), gains, gains),
-        in_specs=[anywhere()] * 2,
+        in_specs=[in_vmem()] * 2,
         out_specs=[anywhere()] * 3,
         scratch_shapes=weight_sems() + [dma((1,)), dma((4,)), dma((4,))],
         compiler_params=pltpu.CompilerParams(collective_id=4, has_side_effects=True),

time: 457 us -> 433 us (0.947)
  Pallas kernels: 414 us -> 391 us
    pallas_call x1, Pallas kernels: 68 us -> 44.5 us  [gather_weights(): pl.pallas_call(weights_kernel, out_shape=(jax.ShapeDtypeStruct((mats, 4,...]
  transfers between devices with their start and end apart: 2 -> 2, of which waited for: 0 -> 0; matrix products, arithmetic and copies ran while one was open for 2% -> 2% of each run, Pallas kernels for 15% -> 10%
where the time goes in v1:
time: 433 us; the launch traced here: 425 us
  Pallas kernels  391 us (90%)
  local copies, waits for them, and re-layouts  17.9 us (4%)
  other arithmetic  14.4 us (3%)
    pallas_call x2, Pallas kernels, backward_layer(): pl.pallas_call(functools.partial(backward_kernel, layer, features), out_s...  143 us
    pallas_call x2, Pallas kernels, forward_layer(): pl.pallas_call(functools.partial(forward_kernel, layer, features), out_sh...  119 us
    pallas_call x1, Pallas kernels, sum_gradients(): pl.pallas_call(functools.partial(gradient_kernel, features), out_shape=fe...  84.3 us
    pallas_call x1, Pallas kernels, gather_weights(): pl.pallas_call(weights_kernel, out_shape=(jax.ShapeDtypeStruct((mats, 4,...  44.5 us
  transfers between devices with their start and end apart: 2, of which 0 were waited for; matrix products, arithmetic and copies ran while one was open for 2% of the time, Pallas kernels for 10%

profile of v1, /device:TPU:0, one launch (start us, length us, event | category | flops | bytes accessed | tf_op | source)
XLA Modules:
  0.0 424.7 jit_solution(4966499704313182206)
XLA Ops:
  0.6 0.0 copy-start
  0.6 0.0 copy-start.9
  0.7 0.1 collective-permute-start
  0.8 0.5 collective-permute-start.1
  1.2 0.1 copy-done
  1.3 0.2 reduce-window.8
  1.5 1.3 pad.4.gain_ref
  2.8 1.8 fusion.12
  4.6 0.0 copy-done.9
  4.6 1.9 pad_maximum_fusion.shard_ref.refs_8_
  6.5 0.0 copy-start.12
  6.5 0.0 copy-start.13
  6.5 44.5 %gather_weights.1 = (bf16[4,4,272,1088]{3,2,1,0:T(8,128)(2,1)}, bf16[4,16,272]{2,1,0:T(8,128)(2,1)}, bf16[4,16,272]{2,1,0:T(8,128)(2,1)}) custom-call(bf16[4,272,1088]{2,1,0:T(8,128)(2,1)} %pad_maximum_fusion.shard_ref.refs_8_, bf16[16,272]{1,0:T(8,128)(2,1)} %pad.4.gain_ref), custom_call_target="tpu_custom_call" | custom-call | bytes 30000000 | tf_op jit(solution)/shard_map/gather_weights/pallas_call | solution.py:943
  51.0 0.8 fusion.9
  51.8 0.7 select_n.68.refs_2_.refs_3_
  52.5 0.7 select_n.72.refs_2_.refs_3_
  53.2 0.1 pad.7.clone
  53.3 0.1 convert_reduce_fusion
  53.4 0.1 convert_reduce_fusion.1
  53.4 0.8 fusion.7.refs_1_
  54.2 0.8 fusion.5.refs_2_
  55.0 0.0 copy-done.12
  55.0 0.0 copy-done.13
  55.0 0.8 dynamic-slice_bitcast_fusion
  55.8 0.0 collective-permute-done.refs_5_.refs_11_
  55.8 0.0 collective-permute-done.1.refs_7_.refs_13_
  55.8 70.4 %layer_forward_0.1 = (bf16[96,1088]{1,0:T(8,128)(2,1)}, f32[96,1088]{1,0:T(8,128)}, bf16[96,1088]{1,0:T(8,128)(2,1)}, bf16[96,1088]{1,0:T(8,128)(2,1)}, bf16[4,9...) custom-call(bf16[96,1088]{1,0:T(8,128)(2,1)} %get-tuple-element.117., ...), custom_call_target="tpu_custom_call" | custom-call | flops 3000000000 | bytes 24000000 | tf_op jit(solution)/shard_map/layer_forward_0/pallas_call | solution.py:513
  126.2 48.7 %layer_forward_1.1 = (bf16[96,1088]{1,0:T(8,128)(2,1)}, f32[96,1088]{1,0:T(8,128)}, bf16[96,1088]{1,0:T(8,128)(2,1)}, bf16[96,1088]{1,0:T(8,128)(2,1)}, bf16[4,9...) custom-call(bf16[96,1088]{1,0:T(8,128)(2,1)} %get-tuple-element.62.r, ...), custom_call_target="tpu_custom_call" | custom-call | flops 3000000000 | bytes 24000000 | tf_op jit(solution)/shard_map/layer_forward_1/pallas_call | solution.py:513
  174.9 47.6 %layer_backward_1.1 = (bf16[96,1088]{1,0:T(8,128)(2,1)}, f32[2,1088]{1,0:T(2,128)}, bf16[4,96,1088]{2,1,0:T(8,128)(2,1)}, bf16[4,96,1088]{2,1,0:T(8,128)(2,1)}, ...) custom-call(bf16[96,1088]{1,0:T(8,128)(2,1)} %get-tuple-element.62.ref, ...), custom_call_target="tpu_custom_call" | custom-call | flops 4000000000 | bytes 24000000 | tf_op jit(solution)/shard_map/layer_backward_1/pallas_call | solution.py:739
  222.5 0.0 copy-start.14
  222.5 95.1 %layer_backward_0.1 = (bf16[96,1088]{1,0:T(8,128)(2,1)}, f32[2,1088]{1,0:T(2,128)}, bf16[4,96,1088]{2,1,0:T(8,128)(2,1)}, bf16[4,96,1088]{2,1,0:T(8,128)(2,1)}, ...) custom-call(bf16[96,1088]{1,0:T(8,128)(2,1)} %get-tuple-element.117., ...), custom_call_target="tpu_custom_call" | custom-call | flops 4000000000 | bytes 24000000 | tf_op jit(solution)/shard_map/layer_backward_0/pallas_call | solution.py:739
  317.6 0.0 copy-done.14
  317.6 1.4 maximum_maximum_fusion.refs_11_
  319.0 0.0 copy-start.4
  319.0 84.3 %sum_gradients.1 = (bf16[2,576,1088]{2,1,0:T(8,128)(2,1)}, bf16[2,320,1088]{2,1,0:T(8,128)(2,1)}, bf16[2,320,1088]{2,1,0:T(8,128)(2,1)}, bf16[2,320,1088]{2,1,0:...) custom-call(bf16[96,1088]{1,0:T(8,128)(2,1)} %get-tuple-element.60.r, ...), custom_call_target="tpu_custom_call" | custom-call | flops 3000000000 | bytes 60000000 | tf_op jit(solution)/shard_map/sum_gradients/pallas_call | solution.py:1438
  403.3 0.0 copy-done.4
  403.3 2.3 broadcast_select_fusion
  405.6 0.0 copy-start.2
  405.6 0.0 copy-start.3
  405.6 2.9 fusion
  408.5 0.0 copy-done.2
  408.5 1.5 copy-done.3
  410.0 0.3 broadcast_select_fusion.1
  410.3 0.0 copy-start.7
  410.3 0.0 copy-start.8
  410.3 2.6 fusion.1
  412.9 0.0 copy-done.7
  412.9 0.5 copy-done.8
  413.4 0.2 fusion.2
  413.6 0.0 copy-start.5
  413.6 0.0 copy-start.6
  413.6 1.2 fusion.11
  414.8 0.6 copy-done.5
  415.4 0.4 copy-done.6
  415.8 0.2 fusion.3
  416.0 1.2 slice_bitcast_fusion.3
  417.2 0.0 copy-start.11
  417.2 4.2 concatenate.7
  421.4 1.4 dynamic-slice_bitcast_fusion.2
  422.8 0.0 copy-done.11
  422.8 0.8 copy.21
  423.5 0.0 copy-done.10
  423.5 0.8 copy.22
  424.3 0.0 copy-done.1
  (7 shorter events, 0.0 us)
Async XLA Ops:
  0.6 0.7 copy-start
  0.6 3.9 copy-start.9
  0.7 55.1 %collective-permute-start = (bf16[1088,1088]{1,0:T(8,128)(2,1)}, bf16[1088,1088]{1,0:T(8,128)(2,1)}, u32[]{:S(2)}, u32[]{:S(2)}) collective-permute-start(bf16[1088,1088]{1,0:T(8,128)(2,1)} %bitcast.43), channel_id=1, source_target_pairs={{0,64},{64,0},{1,65},{65,1},{2,66},{66,2},{3,67},{67,3},{4,68},{68... | collective-permute-start | bytes 7102472 | tf_op jit(solution)/shard_map/ppermute | solution.py:1472
  0.8 55.0 %collective-permute-start.1 = (bf16[1088,1088]{1,0:T(8,128)(2,1)}, bf16[1088,1088]{1,0:T(8,128)(2,1)}, u32[]{:S(2)}, u32[]{:S(2)}) collective-permute-start(bf16[1088,1088]{1,0:T(8,128)(2,1)} %bitcast.48), channel_id=1, source_target_pairs={{0,64},{64,0},{1,65},{65,1},{2,66},{66,2},{3,67},{67,3},{4,68},{68... | collective-permute-start | bytes 7102472 | tf_op jit(solution)/shard_map/ppermute | solution.py:1472
  6.5 48.5 %copy-start.12 = (bf16[2,96,1088]{2,1,0:T(8,128)(2,1)S(1)}, bf16[2,96,1088]{2,1,0:T(8,128)(2,1)}, u32[]{:S(2)}) copy-start(bf16[2,96,1088]{2,1,0:T(8,128)(2,1)} %param.9) | copy-start | bytes 1253380
  6.5 48.5 %copy-start.13 = (bf16[2,96,1088]{2,1,0:T(8,128)(2,1)S(1)}, bf16[2,96,1088]{2,1,0:T(8,128)(2,1)}, u32[]{:S(2)}) copy-start(bf16[2,96,1088]{2,1,0:T(8,128)(2,1)} %param.8) | copy-start | bytes 1253380
  222.5 95.1 %copy-start.14 = (f32[2,1088]{1,0:T(2,128)S(1)}, f32[2,1088]{1,0:T(2,128)}, u32[]{:S(2)}) copy-start(f32[2,1088]{1,0:T(2,128)} %get-tuple-element.95) | copy-start | bytes 26116
  319.0 84.3 %copy-start.4 = (bf16[2,576,1088]{2,1,0:T(8,128)(2,1)S(1)}, bf16[2,576,1088]{2,1,0:T(8,128)(2,1)}, u32[]{:S(2)}) copy-start(bf16[2,576,1088]{2,1,0:T(8,128)(2,1)} %get-tuple-element.106) | copy-start | bytes 7520260
  405.6 2.9 copy-start.2
  405.6 4.4 %copy-start.3 = (bf16[2,576,1088]{2,1,0:T(8,128)(2,1)S(1)}, bf16[2,576,1088]{2,1,0:T(8,128)(2,1)}, u32[]{:S(2)}) copy-start(bf16[2,576,1088]{2,1,0:T(8,128)(2,1)} %get-tuple-element.93.refs_10_) | copy-start | bytes 7520260
  410.3 2.7 copy-start.7
  410.3 3.1 copy-start.8
  413.6 1.8 copy-start.5
  413.6 2.3 copy-start.6
  417.2 5.5 %copy-start.11 = (bf16[2,96,1088]{2,1,0:T(8,128)(2,1)S(1)}, bf16[2,96,1088]{2,1,0:T(8,128)(2,1)}, u32[]{:S(2)}) copy-start(bf16[2,96,1088]{2,1,0:T(8,128)(2,1)} %get-tuple-element.97) | copy-start | bytes 1253380
  417.2 6.3 %copy-start.10 = (bf16[2,96,1088]{2,1,0:T(8,128)(2,1)S(1)}, bf16[2,96,1088]{2,1,0:T(8,128)(2,1)}, u32[]{:S(2)}) copy-start(bf16[2,96,1088]{2,1,0:T(8,128)(2,1)} %get-tuple-element.98) | copy-start | bytes 1253380
  417.2 7.1 %copy-start.1 = (s32[2,4]{1,0:T(2,128)S(1)}, s32[2,4]{1,0:T(2,128)}, u32[]{:S(2)}) copy-start(s32[2,4]{1,0:T(2,128)} %param.10) | copy-start | bytes 100
